TPU v7x, 128 devices: a whole 4x4x4 slice. The times are simulated.
128 devices in a mesh: pair: 2 (over x_hi), day: 16 (over z, y), lag: 4 (over x_lo, core).
Axes of the slice: x: 4 (x_hi: 2, x_lo: 2; x = x_hi * 2 + x_lo), y: 4, z: 4, core: 2. Of those that a mesh axis runs over, the one named last changes fastest.
Arguments:
- corr: bfloat16 [2048, 64, 2048], P('pair', 'day', 'lag'), may hold values from -150 to 150
Outputs:
- pws_stack: float32 [2048, 2048], P('pair', 'lag')
- robust_stack: float32 [2048, 2048], P('pair', 'lag')
- day_weights: float32 [2048, 64], P('pair', 'day')
All inputs are finite; a program needn't handle non-finite values.
Results may differ from a plain program's by a relative error of at most 0.00049.
Values may be sent and summed in bfloat16 or wider, within the bound.
A program may use at most 128 MiB of HBM per device.

v0:
```python
import jax
import jax.numpy as jnp
from jax import lax
from jax.sharding import PartitionSpec as P

ITERS = 3
epsilon = 1e-06


def kernel_block(rows, cols, lags):
    offset = (cols[None, :] - rows[:, None]) % lags
    odd = offset % 2 == 1
    angle = jnp.pi * offset.astype(jnp.float32) / lags
    value = jnp.where(odd, 2.0 / lags * jnp.cos(angle) / jnp.where(odd, jnp.sin(angle), 1.0), 0.0)
    return value.astype(jnp.bfloat16)


def per_device(corr):
    width_in = corr.shape[2]
    lags = width_in * lax.axis_size("lag")
    pairs, days_here, width = corr.shape
    days = days_here * lax.axis_size("day")
    data = corr.astype(jnp.float32)
    squares = jnp.sum(data * data, axis=2)
    norm2 = lax.psum(squares, "lag")
    rms = jnp.sqrt(norm2 / lags + epsilon)
    xn = data / rms[:, :, None]
    local_lags = lax.axis_index("lag") * width + jnp.arange(width, dtype=jnp.int32)
    piece = lax.all_gather(corr, "lag", axis=2, tiled=True)
    count = piece.shape[2]
    rows = jnp.arange(count, dtype=jnp.int32)
    block = kernel_block(rows, local_lags, lags)
    quad = jnp.dot(
        piece.reshape(pairs * days_here, count), block, preferred_element_type=jnp.float32
    )
    quad = quad.reshape(pairs, days_here, width)
    den = jnp.maximum(jnp.sqrt(data * data + quad * quad), 0.1 * rms[:, :, None])
    cosine = data / den
    sine = quad / den
    linear, csum, ssum = lax.psum(
        (jnp.sum(xn, axis=1), jnp.sum(cosine, axis=1), jnp.sum(sine, axis=1)), "day"
    )
    pws = linear / days * ((csum * csum + ssum * ssum) / (days * days))
    stack = pws
    for step in range(ITERS):
        energy = jnp.sum(stack * stack, axis=1)
        msq = lax.psum(energy, "lag") / lags
        normed = stack / jnp.sqrt(msq + epsilon)[:, None]
        inner = jnp.sum(xn * normed[:, None, :], axis=2)
        coh = lax.psum(inner, "lag") / lags
        spread = jnp.sum((xn - coh[:, :, None] * normed[:, None, :]) ** 2, axis=2)
        res = lax.psum(spread, "lag") / lags
        rbar = lax.psum(jnp.sum(res, axis=1), "day") / days
        weight = (0.1 + jnp.abs(coh)) / (res + rbar[:, None] + epsilon)
        stack, total = lax.psum(
            (jnp.sum(weight[:, :, None] * xn, axis=1), jnp.sum(weight, axis=1)), "day"
        )
    robust = stack / total[:, None]
    shares = weight / total[:, None]
    return (pws, robust, shares)


def solution(mesh):
    return jax.shard_map(
        per_device,
        mesh=mesh,
        in_specs=(P("pair", "day", "lag"),),
        out_specs=(P("pair", "lag"), P("pair", "lag"), P("pair", "day")),
        check_vma=False,
    )
```

profile of v0, /device:TPU:0, one launch (start us, length us, event | category | flops | bytes accessed | tf_op | source)
XLA Modules:
  0.0 961.6 jit_solution(4867787955644400862)
XLA Ops:
  7.2 0.0 all-gather.2.cloned.1.call-start
  7.2 0.7 all-gather.2.cloned.1.call-update
  7.9 0.0 all-reduce.12.cloned.1.call-start
  7.9 4.5 fusion.1
  12.4 17.1 %psum.140 = f32[1024,4]{1,0:T(8,128)S(1)} all-reduce(f32[1024,4]{1,0:T(8,128)S(1)} %fusion.1), channel_id=1, replica_groups=mesh['pair'=2,'day'=16,'lag'=4] {'lag'}, use_global_device_ids=true, to_apply=%region_1.0 | all-reduce | flops 4096 | bytes 32768 | tf_op jit(solution)/shard_map/psum | solution.py:25
  29.5 0.2 add_sqrt_fusion
  29.7 19.0 %select_convert_fusion.4 = bf16[2048,512]{1,0:T(8,128)(2,1)S(1)} fusion(s32[512]{0:T(512)S(1)} %iota_add_fusion), kind=kLoop, calls=%fused_computation.28.clone.clone.1 | loop fusion | flops 32505856 | bytes 2099200 | tf_op jit(solution)/shard_map/dot_general | solution.py:33
  48.8 113.7 %all-gather.2.cloned.1.call-done = bf16[1024,4,2048]{2,1,0:T(4,128)(2,1)} async-done(((bf16[1024,4,512]{2,1,0:T(4,128)(2,1)}), bf16[1024,4,2048]{2,1,0:T(4,128)(2,1)}) %all-gather.2.cloned.1.call-update) | async-done | bytes 16777232 | tf_op jit(solution)/shard_map/all_gather | solution.py:29
  162.5 23.7 %reshape.35 = bf16[4096,2048]{1,0:T(8,128)(2,1)} reshape(bf16[1024,4,2048]{2,1,0:T(4,128)(2,1)} %all-gather.2.cloned.1.call-done) | data formatting | bytes 33554432 | tf_op jit(solution)/shard_map/reshape | solution.py:34
  186.1 14.5 %convolution_bitcast_fusion = f32[4096,512]{0,1:T(8,128)} fusion(bf16[4096,2048]{1,0:T(8,128)(2,1)} %reshape.35, bf16[2048,512]{1,0:T(8,128)(2,1)S(1)} %select_convert_fusion.4), kind=kOutput, calls=%fused_computation.18 | convolution fusion | flops 8589934592 | bytes 27262976 | tf_op jit(solution)/shard_map/dot_general | solution.py:33
  200.7 9.0 copy.24
  209.7 9.8 %reshape.36 = f32[1024,4,512]{2,1,0:T(4,128)} reshape(f32[4096,512]{1,0:T(8,128)} %copy.24) | data formatting | bytes 16777216 | tf_op jit(solution)/shard_map/reshape | solution.py:36
  219.5 32.9 %fusion.34 = (f32[1024,512]{1,0:T(8,128)}, f32[1024,4,512]{2,1,0:T(4,128)}, f32[1024,512]{1,0:T(8,128)}, f32[1024,512]{1,0:T(8,128)}) fusion(f32[1024,4]{1,0:T(8,128)S(1)} %get-tuple-element.19, bf16[1024,4,512]{2,1,0:T(4,128)(2,1)} %param.1, f32[1024,4,512]{2,1,0:T(4,128)} %reshape.36, f32[1024,4]{1,0:T(8,128)S(1)} %get-tuple-element.20), kind=kLoop, calls=%fused_computation.82 | loop fusion | flops 21495808 | bytes 27295744 | tf_op jit(solution)/shard_map/reduce_sum | solution.py:41
  252.4 0.0 all-reduce.12.cloned.1.call-update
  252.4 0.0 all-reduce.6.cloned.1.call-start
  252.5 125.8 %all-reduce.12.cloned.1.call-done = (f32[1024,512]{1,0:T(8,128)}, f32[1024,512]{1,0:T(8,128)}, f32[1024,512]{1,0:T(8,128)}) async-done(((f32[1024,512]{1,0:T(8,128)}, f32[1024,512]{1,0:T(8,128)}, f32[1024,512]{1,0:T(8,128)}), (f32[1024,512]{1,0:T(8,128)}, f32[1024,512]{1,0:T(8,128)}, f32[1024,512]{1,0:T(8,128)})) %all-reduce.12.cloned.1.call-update) | async-done | bytes 6291472 | tf_op jit(solution)/shard_map/psum | solution.py:40
  378.3 4.7 multiply_reduce_fusion.11
  383.0 6.8 psum.144
  389.8 1.8 broadcast_divide_fusion.3
  391.6 5.7 multiply_reduce_fusion.8
  397.3 16.0 %psum.145 = f32[1024,4]{1,0:T(8,128)S(1)} all-reduce(f32[1024,4]{1,0:T(8,128)S(1)} %multiply_reduce_fusion.8), channel_id=1, replica_groups=mesh['pair'=2,'day'=16,'lag'=4] {'lag'}, use_global_device_ids=true, to_apply=%region_11.12 | all-reduce | flops 4096 | bytes 32768 | tf_op jit(solution)/shard_map/psum | solution.py:50
  413.4 7.1 multiply_reduce_fusion.7
  420.5 16.3 %psum.146 = f32[1024,4]{1,0:T(8,128)S(1)} all-reduce(f32[1024,4]{1,0:T(8,128)S(1)} %multiply_reduce_fusion.7), channel_id=1, replica_groups=mesh['pair'=2,'day'=16,'lag'=4] {'lag'}, use_global_device_ids=true, to_apply=%region_13.14 | all-reduce | flops 4096 | bytes 32768 | tf_op jit(solution)/shard_map/psum | solution.py:52
  436.8 0.2 multiply_reduce_fusion.14
  437.0 38.4 %psum.147 = f32[1024]{0:T(1024)S(1)} all-reduce(f32[1024]{0:T(1024)S(1)} %multiply_reduce_fusion.14), channel_id=1, replica_groups=mesh['pair'=2,'day'=16,'lag'=4] {'day'}, use_global_device_ids=true, to_apply=%region_15.16 | all-reduce | flops 1024 | bytes 8192 | tf_op jit(solution)/shard_map/psum | solution.py:53
  475.5 0.2 add_divide_fusion.1
  475.7 9.3 multiply_reduce_fusion.6
  485.0 0.0 all-reduce.6.cloned.1.call-update
  485.0 0.0 all-reduce.8.cloned.1.call-start
  485.1 86.2 %all-reduce.6.cloned.1.call-done = f32[1024,512]{1,0:T(8,128)} async-done(((f32[1024,512]{1,0:T(8,128)}), f32[1024,512]{1,0:T(8,128)}) %all-reduce.6.cloned.1.call-update) | async-done | bytes 2097168 | tf_op jit(solution)/shard_map/psum | solution.py:55
  571.3 1.8 multiply_reduce_fusion.10
  573.1 5.8 psum.149
  579.0 1.8 broadcast_divide_fusion.2
  580.8 5.7 multiply_reduce_fusion.5
  586.4 16.7 %psum.150 = f32[1024,4]{1,0:T(8,128)S(1)} all-reduce(f32[1024,4]{1,0:T(8,128)S(1)} %multiply_reduce_fusion.5), channel_id=1, replica_groups=mesh['pair'=2,'day'=16,'lag'=4] {'lag'}, use_global_device_ids=true, to_apply=%region_21.22 | all-reduce | flops 4096 | bytes 32768 | tf_op jit(solution)/shard_map/psum | solution.py:50
  603.2 7.1 multiply_reduce_fusion.4
  610.4 16.4 %psum.151 = f32[1024,4]{1,0:T(8,128)S(1)} all-reduce(f32[1024,4]{1,0:T(8,128)S(1)} %multiply_reduce_fusion.4), channel_id=1, replica_groups=mesh['pair'=2,'day'=16,'lag'=4] {'lag'}, use_global_device_ids=true, to_apply=%region_23.24 | all-reduce | flops 4096 | bytes 32768 | tf_op jit(solution)/shard_map/psum | solution.py:52
  626.7 0.2 multiply_reduce_fusion.13
  626.9 38.2 %psum.152 = f32[1024]{0:T(1024)S(1)} all-reduce(f32[1024]{0:T(1024)S(1)} %multiply_reduce_fusion.13), channel_id=1, replica_groups=mesh['pair'=2,'day'=16,'lag'=4] {'day'}, use_global_device_ids=true, to_apply=%region_25.26 | all-reduce | flops 1024 | bytes 8192 | tf_op jit(solution)/shard_map/psum | solution.py:53
  665.1 0.2 add_divide_fusion
  665.3 9.3 multiply_reduce_fusion.3
  674.6 0.0 all-reduce.8.cloned.1.call-update
  674.7 0.0 all-reduce.10.cloned.1.call-start
  674.7 86.7 %all-reduce.8.cloned.1.call-done = f32[1024,512]{1,0:T(8,128)} async-done(((f32[1024,512]{1,0:T(8,128)}), f32[1024,512]{1,0:T(8,128)}) %all-reduce.8.cloned.1.call-update) | async-done | bytes 2097168 | tf_op jit(solution)/shard_map/psum | solution.py:55
  761.4 1.8 multiply_reduce_fusion.9
  763.2 5.7 psum.154
  768.9 1.8 broadcast_divide_fusion.1
  770.7 5.7 multiply_reduce_fusion.2
  776.4 16.7 %psum.155 = f32[1024,4]{1,0:T(8,128)S(1)} all-reduce(f32[1024,4]{1,0:T(8,128)S(1)} %multiply_reduce_fusion.2), channel_id=1, replica_groups=mesh['pair'=2,'day'=16,'lag'=4] {'lag'}, use_global_device_ids=true, to_apply=%region_31.32 | all-reduce | flops 4096 | bytes 32768 | tf_op jit(solution)/shard_map/psum | solution.py:50
  793.2 7.1 multiply_reduce_fusion.1
  800.3 16.6 %psum.156 = f32[1024,4]{1,0:T(8,128)S(1)} all-reduce(f32[1024,4]{1,0:T(8,128)S(1)} %multiply_reduce_fusion.1), channel_id=1, replica_groups=mesh['pair'=2,'day'=16,'lag'=4] {'lag'}, use_global_device_ids=true, to_apply=%region_33.34 | all-reduce | flops 4096 | bytes 32768 | tf_op jit(solution)/shard_map/psum | solution.py:52
  816.9 0.2 multiply_reduce_fusion.12
  817.1 38.2 %psum.157 = f32[1024]{0:T(1024)S(1)} all-reduce(f32[1024]{0:T(1024)S(1)} %multiply_reduce_fusion.12), channel_id=1, replica_groups=mesh['pair'=2,'day'=16,'lag'=4] {'day'}, use_global_device_ids=true, to_apply=%region_35.36 | all-reduce | flops 1024 | bytes 8192 | tf_op jit(solution)/shard_map/psum | solution.py:53
  855.3 0.4 fusion.32
  855.6 9.3 multiply_reduce_fusion
  864.9 0.0 all-reduce.10.cloned.1.call-update
  865.0 35.7 %psum.159 = f32[1024]{0:T(1024)S(1)} all-reduce(f32[1024]{0:T(1024)S(1)} %get-tuple-element.11), channel_id=1, replica_groups=mesh['pair'=2,'day'=16,'lag'=4] {'day'}, use_global_device_ids=true, to_apply=%region_39.40 | all-reduce | flops 1024 | bytes 8192 | tf_op jit(solution)/shard_map/psum | solution.py:55
  900.6 0.3 multiply_divide_fusion
  901.0 0.8 copy.25
  901.8 50.0 %all-reduce.10.cloned.1.call-done = f32[1024,512]{1,0:T(8,128)} async-done(((f32[1024,512]{1,0:T(8,128)}), f32[1024,512]{1,0:T(8,128)}) %all-reduce.10.cloned.1.call-update) | async-done | bytes 2097168 | tf_op jit(solution)/shard_map/psum | solution.py:55
  951.8 3.1 broadcast_divide_fusion
  (10 shorter events, 0.2 us)
Async XLA Ops:
  7.2 155.3 %all-gather.2.cloned.1.call-start = ((), (), s32[]{:S(2)}) async-start(), calls=%async_computation | async-start | bytes 20971520 | tf_op jit(solution)/shard_map/all_gather | solution.py:29
  7.9 370.4 %all-reduce.12.cloned.1.call-start = ((), (), s32[]{:S(2)}) async-start(), calls=%async_computation.4 | async-start | bytes 12582912 | tf_op jit(solution)/shard_map/psum | solution.py:40
  252.4 318.9 %all-reduce.6.cloned.1.call-start = ((), (), s32[]{:S(2)}) async-start(), calls=%async_computation.1 | async-start | bytes 4194304 | tf_op jit(solution)/shard_map/psum | solution.py:55
  485.0 276.4 %all-reduce.8.cloned.1.call-start = ((), (), s32[]{:S(2)}) async-start(), calls=%async_computation.2 | async-start | bytes 4194304 | tf_op jit(solution)/shard_map/psum | solution.py:55
  674.7 277.1 %all-reduce.10.cloned.1.call-start = ((), (), s32[]{:S(2)}) async-start(), calls=%async_computation.3 | async-start | bytes 4194304 | tf_op jit(solution)/shard_map/psum | solution.py:55
Sparse Core Ops, SparseCore 0:
  9.6 152.7 all-gather.1
  252.6 125.6 all-reduce.11
  485.1 86.1 all-reduce.5
  674.8 86.5 all-reduce.7
  865.1 86.6 all-reduce.9
where the time goes:
time: 972 us; the launch traced here: 962 us
  waiting for transfers between devices  463 us (48%)
  blocking collectives  285 us (29%)
  other arithmetic  142 us (15%)
  local copies, waits for them, and re-layouts  43.3 us (4%)
  matrix products  14.5 us (1%)
  between operations  14.2 us (1%)
    psum x3, waiting for transfers between devices, per_device(): lax.psum((jnp.sum(weight[:, :, None] * xn, axis=1), jnp.sum(weight, axis=...  223 us
    psum x1, waiting for transfers between devices, per_device(): lax.psum((jnp.sum(xn, axis=1), jnp.sum(cosine, axis=1), jnp.sum(sine, axi...  126 us
    psum x3, blocking collectives, per_device(): rbar = lax.psum(jnp.sum(res, axis=1), 'day') / days  115 us
    all_gather x1, waiting for transfers between devices, per_device(): piece = lax.all_gather(corr, 'lag', axis=2, tiled=True)  114 us
    psum x3, blocking collectives, per_device(): coh = lax.psum(inner, 'lag') / lags  49.5 us
    psum x3, blocking collectives, per_device(): res = lax.psum(spread, 'lag') / lags  49.3 us
    psum x1, blocking collectives, per_device(): lax.psum((jnp.sum(weight[:, :, None] * xn, axis=1), jnp.sum(weight, axis=...  35.7 us
    reduce_sum x1, other arithmetic, per_device(): jnp.sum(xn, axis=1)  32.9 us
  transfers between devices with their start and end apart: 5, of which 5 were waited for; matrix products, arithmetic and copies ran while one was open for 3% of the time, Pallas kernels for 0%

commit v1 on v0

--- a/solution.py
+++ b/solution.py
@@ -49,7 +49,7 @@
         inner = jnp.sum(xn * normed[:, None, :], axis=2)
         coh = lax.psum(inner, "lag") / lags
         spread = jnp.sum((xn - coh[:, :, None] * normed[:, None, :]) ** 2, axis=2)
-        res = lax.psum(spread, "lag") / lags
+        res = jnp.sum(lax.all_gather(spread, "lag"), axis=0) / lags
         rbar = lax.psum(jnp.sum(res, axis=1), "day") / days
         weight = (0.1 + jnp.abs(coh)) / (res + rbar[:, None] + epsilon)
         stack, total = lax.psum(

time: 972 us -> 942 us (0.969)
  blocking collectives: 285 us -> 249 us
    psum x3 -> x0, blocking collectives: 49.3 us -> none  [per_device(): res = lax.psum(spread, 'lag') / lags]
    all_gather x0 -> x3, blocking collectives: none -> 35.8 us  [per_device(): res = jnp.sum(lax.all_gather(spread, 'lag'), axis=0) / lags]
    psum x3, blocking collectives: 49.5 us -> 32.1 us  [per_device(): coh = lax.psum(inner, 'lag') / lags]
where the time goes in v1:
time: 942 us; the launch traced here: 932 us
  waiting for transfers between devices  467 us (50%)
  blocking collectives  249 us (26%)
  other arithmetic  140 us (15%)
  local copies, waits for them, and re-layouts  46.4 us (5%)
  matrix products  14.5 us (2%)
  between operations  14.2 us (2%)
    psum x3, waiting for transfers between devices, per_device(): lax.psum((jnp.sum(weight[:, :, None] * xn, axis=1), jnp.sum(weight, axis=...  223 us
    psum x1, waiting for transfers between devices, per_device(): lax.psum((jnp.sum(xn, axis=1), jnp.sum(cosine, axis=1), jnp.sum(sine, axi...  126 us
    all_gather x1, waiting for transfers between devices, per_device(): piece = lax.all_gather(corr, 'lag', axis=2, tiled=True)  118 us
    psum x3, blocking collectives, per_device(): rbar = lax.psum(jnp.sum(res, axis=1), 'day') / days  115 us
    psum x1, blocking collectives, per_device(): lax.psum((jnp.sum(weight[:, :, None] * xn, axis=1), jnp.sum(weight, axis=...  35.9 us
    all_gather x3, blocking collectives, per_device(): res = jnp.sum(lax.all_gather(spread, 'lag'), axis=0) / lags  35.8 us
    reduce_sum x1, other arithmetic, per_device(): jnp.sum(xn, axis=1)  32.9 us
    psum x3, blocking collectives, per_device(): coh = lax.psum(inner, 'lag') / lags  32.1 us
  transfers between devices with their start and end apart: 5, of which 5 were waited for; matrix products, arithmetic and copies ran while one was open for 3% of the time, Pallas kernels for 0%

profile of v1, /device:TPU:0, one launch (start us, length us, event | category | flops | bytes accessed | tf_op | source)
XLA Modules:
  0.0 931.8 jit_solution(5019561756902357447)
XLA Ops:
  7.2 0.0 all-gather.5.cloned.1.call-start
  7.2 0.7 all-gather.5.cloned.1.call-update
  7.9 0.0 all-reduce.12.cloned.1.call-start
  7.9 4.5 fusion.1
  12.4 0.2 copy.95
  12.6 11.3 %psum.119 = f32[1024,4]{0,1:T(4,128)S(1)} all-reduce(f32[1024,4]{0,1:T(4,128)S(1)} %copy.95), channel_id=1, replica_groups=mesh['pair'=2,'day'=16,'lag'=4] {'lag'}, use_global_device_ids=true, to_apply=%region_1.0 | all-reduce | flops 4096 | bytes 32768 | tf_op jit(solution)/shard_map/psum | solution.py:25
  23.9 0.2 copy.96
  24.1 0.2 copy.98
  24.4 19.0 %select_convert_fusion.4 = bf16[2048,512]{1,0:T(8,128)(2,1)S(1)} fusion(s32[512]{0:T(512)S(1)} %iota_add_fusion), kind=kLoop, calls=%fused_computation.28.clone.clone.1 | loop fusion | flops 32505856 | bytes 2099200 | tf_op jit(solution)/shard_map/dot_general | solution.py:33
  43.4 117.9 %all-gather.5.cloned.1.call-done = bf16[1024,4,2048]{2,1,0:T(4,128)(2,1)} async-done(((bf16[1024,4,512]{2,1,0:T(4,128)(2,1)}), bf16[1024,4,2048]{2,1,0:T(4,128)(2,1)}) %all-gather.5.cloned.1.call-update) | async-done | bytes 16777232 | tf_op jit(solution)/shard_map/all_gather | solution.py:29
  161.3 23.7 %reshape.35 = bf16[4096,2048]{1,0:T(8,128)(2,1)} reshape(bf16[1024,4,2048]{2,1,0:T(4,128)(2,1)} %all-gather.5.cloned.1.call-done) | data formatting | bytes 33554432 | tf_op jit(solution)/shard_map/reshape | solution.py:34
  185.0 14.5 %convolution_bitcast_fusion = f32[4096,512]{0,1:T(8,128)} fusion(bf16[4096,2048]{1,0:T(8,128)(2,1)} %reshape.35, bf16[2048,512]{1,0:T(8,128)(2,1)S(1)} %select_convert_fusion.4), kind=kOutput, calls=%fused_computation.18 | convolution fusion | flops 8589934592 | bytes 27262976 | tf_op jit(solution)/shard_map/dot_general | solution.py:33
  199.5 9.0 copy.97
  208.5 9.8 %reshape.36 = f32[1024,4,512]{2,1,0:T(4,128)} reshape(f32[4096,512]{1,0:T(8,128)} %copy.97) | data formatting | bytes 16777216 | tf_op jit(solution)/shard_map/reshape | solution.py:36
  218.3 32.9 %fusion.34 = (f32[1024,512]{1,0:T(8,128)}, f32[1024,4,512]{2,1,0:T(4,128)}, f32[1024,512]{1,0:T(8,128)}, f32[1024,512]{1,0:T(8,128)}) fusion(f32[1024,4]{1,0:T(8,128)S(1)} %copy.96, bf16[1024,4,512]{2,1,0:T(4,128)(2,1)} %param.1, f32[1024,4,512]{2,1,0:T(4,128)} %reshape.36, f32[1024,4]{1,0:T(8,128)S(1)} %copy.98), kind=kLoop, calls=%fused_computation.82 | loop fusion | flops 21495808 | bytes 27295744 | tf_op jit(solution)/shard_map/reduce_sum | solution.py:41
  251.3 0.0 all-reduce.6.cloned.1.call-start
  251.3 125.7 %all-reduce.12.cloned.1.call-done = (f32[1024,512]{1,0:T(8,128)}, f32[1024,512]{1,0:T(8,128)}, f32[1024,512]{1,0:T(8,128)}) async-done(((f32[1024,512]{1,0:T(8,128)}, f32[1024,512]{1,0:T(8,128)}, f32[1024,512]{1,0:T(8,128)}), (f32[1024,512]{1,0:T(8,128)}, f32[1024,512]{1,0:T(8,128)}, f32[1024,512]{1,0:T(8,128)})) %all-reduce.12.cloned.1.call-update) | async-done | bytes 6291472 | tf_op jit(solution)/shard_map/psum | solution.py:40
  377.0 4.7 multiply_reduce_fusion.11
  381.7 6.8 psum.123
  388.5 1.8 broadcast_divide_fusion.3
  390.4 5.7 multiply_reduce_fusion.8
  396.0 0.2 copy.99
  396.2 10.2 %psum.124 = f32[1024,4]{0,1:T(4,128)S(1)} all-reduce(f32[1024,4]{0,1:T(4,128)S(1)} %copy.99), channel_id=1, replica_groups=mesh['pair'=2,'day'=16,'lag'=4] {'lag'}, use_global_device_ids=true, to_apply=%region_11.12 | all-reduce | flops 4096 | bytes 32768 | tf_op jit(solution)/shard_map/psum | solution.py:50
  406.4 0.2 copy.100
  406.7 7.1 multiply_reduce_fusion.7
  413.8 0.2 copy.101
  414.0 5.2 all-gather
  419.3 38.4 %psum.125 = f32[1024]{0:T(1024)S(1)} all-reduce(f32[1024]{0:T(1024)S(1)} %multiply_reduce_fusion.14), channel_id=1, replica_groups=mesh['pair'=2,'day'=16,'lag'=4] {'day'}, use_global_device_ids=true, to_apply=%region_15.16 | all-reduce | flops 1024 | bytes 8192 | tf_op jit(solution)/shard_map/psum | solution.py:53
  457.7 0.2 copy.103
  458.0 9.3 multiply_reduce_fusion.6
  467.3 0.0 all-reduce.8.cloned.1.call-start
  467.3 86.3 %all-reduce.6.cloned.1.call-done = f32[1024,512]{1,0:T(8,128)} async-done(((f32[1024,512]{1,0:T(8,128)}), f32[1024,512]{1,0:T(8,128)}) %all-reduce.6.cloned.1.call-update) | async-done | bytes 2097168 | tf_op jit(solution)/shard_map/psum | solution.py:55
  553.7 1.8 multiply_reduce_fusion.10
  555.5 5.8 psum.127
  561.3 1.8 broadcast_divide_fusion.2
  563.1 5.7 multiply_reduce_fusion.5
  568.8 0.2 copy.104
  569.0 10.9 %psum.128 = f32[1024,4]{0,1:T(4,128)S(1)} all-reduce(f32[1024,4]{0,1:T(4,128)S(1)} %copy.104), channel_id=1, replica_groups=mesh['pair'=2,'day'=16,'lag'=4] {'lag'}, use_global_device_ids=true, to_apply=%region_21.22 | all-reduce | flops 4096 | bytes 32768 | tf_op jit(solution)/shard_map/psum | solution.py:50
  579.9 0.2 copy.105
  580.1 7.1 multiply_reduce_fusion.4
  587.3 15.2 %all-gather.1 = f32[4096,4]{1,0:T(8,128)S(1)} all-gather(f32[1024,4]{1,0:T(8,128)S(1)} %multiply_reduce_fusion.4), channel_id=3, replica_groups=mesh['pair'=2,'day'=16,'lag'=4] {'lag'}, dimensions={0}, use_global_device_ids=true | all-gather | bytes 81920 | tf_op jit(solution)/shard_map/all_gather | solution.py:52
  602.4 0.6 copy.106
  603.1 38.5 %psum.129 = f32[1024]{0:T(1024)S(1)} all-reduce(f32[1024]{0:T(1024)S(1)} %multiply_reduce_fusion.13), channel_id=1, replica_groups=mesh['pair'=2,'day'=16,'lag'=4] {'day'}, use_global_device_ids=true, to_apply=%region_25.26 | all-reduce | flops 1024 | bytes 8192 | tf_op jit(solution)/shard_map/psum | solution.py:53
  641.6 0.2 copy.107
  641.8 9.3 multiply_reduce_fusion.3
  651.2 0.0 all-reduce.10.cloned.1.call-start
  651.2 86.6 %all-reduce.8.cloned.1.call-done = f32[1024,512]{1,0:T(8,128)} async-done(((f32[1024,512]{1,0:T(8,128)}), f32[1024,512]{1,0:T(8,128)}) %all-reduce.8.cloned.1.call-update) | async-done | bytes 2097168 | tf_op jit(solution)/shard_map/psum | solution.py:55
  737.8 1.8 multiply_reduce_fusion.9
  739.6 5.7 psum.131
  745.3 1.8 broadcast_divide_fusion.1
  747.1 5.7 multiply_reduce_fusion.2
  752.7 0.2 copy.108
  752.9 10.9 %psum.132 = f32[1024,4]{0,1:T(4,128)S(1)} all-reduce(f32[1024,4]{0,1:T(4,128)S(1)} %copy.108), channel_id=1, replica_groups=mesh['pair'=2,'day'=16,'lag'=4] {'lag'}, use_global_device_ids=true, to_apply=%region_31.32 | all-reduce | flops 4096 | bytes 32768 | tf_op jit(solution)/shard_map/psum | solution.py:50
  763.8 0.2 copy.109
  764.1 7.1 multiply_reduce_fusion.1
  771.2 15.4 %all-gather.2 = f32[4096,4]{1,0:T(8,128)S(1)} all-gather(f32[1024,4]{1,0:T(8,128)S(1)} %multiply_reduce_fusion.1), channel_id=4, replica_groups=mesh['pair'=2,'day'=16,'lag'=4] {'lag'}, dimensions={0}, use_global_device_ids=true | all-gather | bytes 81920 | tf_op jit(solution)/shard_map/all_gather | solution.py:52
  786.6 0.6 copy.110
  787.3 38.5 %psum.133 = f32[1024]{0:T(1024)S(1)} all-reduce(f32[1024]{0:T(1024)S(1)} %multiply_reduce_fusion.12), channel_id=1, replica_groups=mesh['pair'=2,'day'=16,'lag'=4] {'day'}, use_global_device_ids=true, to_apply=%region_35.36 | all-reduce | flops 1024 | bytes 8192 | tf_op jit(solution)/shard_map/psum | solution.py:53
  825.8 0.2 copy.111
  826.0 9.3 multiply_reduce_fusion
  835.3 35.9 %psum.135 = f32[1024]{0:T(1024)S(1)} all-reduce(f32[1024]{0:T(1024)S(1)} %get-tuple-element.20), channel_id=1, replica_groups=mesh['pair'=2,'day'=16,'lag'=4] {'day'}, use_global_device_ids=true, to_apply=%region_39.40 | all-reduce | flops 1024 | bytes 8192 | tf_op jit(solution)/shard_map/psum | solution.py:55
  871.2 0.6 multiply_divide_fusion
  871.8 50.1 %all-reduce.10.cloned.1.call-done = f32[1024,512]{1,0:T(8,128)} async-done(((f32[1024,512]{1,0:T(8,128)}), f32[1024,512]{1,0:T(8,128)}) %all-reduce.10.cloned.1.call-update) | async-done | bytes 2097168 | tf_op jit(solution)/shard_map/psum | solution.py:55
  921.9 3.1 broadcast_divide_fusion
  (24 shorter events, 0.4 us)
Async XLA Ops:
  7.2 154.1 %all-gather.5.cloned.1.call-start = ((), (), s32[]{:S(2)}) async-start(), calls=%async_computation | async-start | bytes 20971520 | tf_op jit(solution)/shard_map/all_gather | solution.py:29
  7.9 369.1 %all-reduce.12.cloned.1.call-start = ((), (), s32[]{:S(2)}) async-start(), calls=%async_computation.4 | async-start | bytes 12582912 | tf_op jit(solution)/shard_map/psum | solution.py:40
  251.3 302.4 %all-reduce.6.cloned.1.call-start = ((), (), s32[]{:S(2)}) async-start(), calls=%async_computation.1 | async-start | bytes 4194304 | tf_op jit(solution)/shard_map/psum | solution.py:55
  467.3 270.5 %all-reduce.8.cloned.1.call-start = ((), (), s32[]{:S(2)}) async-start(), calls=%async_computation.2 | async-start | bytes 4194304 | tf_op jit(solution)/shard_map/psum | solution.py:55
  651.2 270.8 %all-reduce.10.cloned.1.call-start = ((), (), s32[]{:S(2)}) async-start(), calls=%async_computation.3 | async-start | bytes 4194304 | tf_op jit(solution)/shard_map/psum | solution.py:55
Sparse Core Ops, SparseCore 0:
  9.6 151.6 all-gather.4
  251.4 125.5 all-reduce.11
  467.4 86.2 all-reduce.5
  651.3 86.4 all-reduce.7
  835.5 86.4 all-reduce.9
